TPU v7x, 32 devices: a whole 2x2x4 slice. The times are simulated.
32 devices in a mesh: team: 8 (over y, x, core), rep: 4 (over z).
Axes of the slice: x: 2, y: 2, z: 4, core: 2. Of those that a mesh axis runs over, the one named last changes fastest.
Arguments:
- features: bfloat16 [1024, 1024], P(('team', 'rep')), may hold values from -6 to 6
- degree: int32 [1024], P(('team', 'rep')), may hold values from 4 to 16
- blocks: bfloat16 [8, 4, 2, 128, 128], P('team', 'rep'), may hold values from -3 to 3
- block_cols: int32 [8, 4, 2], P('team', 'rep'), may hold values from 0 to 1, each once within a row
- block_count: int32 [8, 4], P('team', 'rep'), may hold values from 1 to 2, as said below
Outputs:
- hop1: bfloat16 [1024, 1024], P(('team', 'rep'))
- hop2: bfloat16 [1024, 1024], P(('team', 'rep'))
- hop3: bfloat16 [1024, 1024], P(('team', 'rep'))
Inputs may be any that keep to these rules, and one draw needn't show every extreme that they name: Each of the 2 entries of a row of block_cols names a different column block; only the first block_count entries are used. `block_count`: some block row of some replica uses all 2 of its blocks.
All inputs are finite; a program needn't handle non-finite values.
Results may differ from a plain program's by a relative error of at most 0.04.
Values may be sent and summed in bfloat16 or wider, within the bound.
A program may use at most 64 MiB of HBM per device.

v0:
```python
import jax
import jax.numpy as jnp
from jax import lax
from jax.sharding import PartitionSpec as P

HOPS = 3


def on_device(features, degree, blocks, block_cols, block_count):
    width = features.shape[1]
    block_size = blocks.shape[-1]
    row_blocks = blocks.shape[0]
    col_blocks = blocks.shape[2]
    panel = row_blocks * block_size
    tiles = blocks[:, 0]
    columns_used = block_cols[:, 0]
    counts_used = block_count[:, 0]
    scale = lax.rsqrt(degree.astype(jnp.float32))[:, None]
    current = features
    results = []
    for hop in range(HOPS):
        sent = (scale * current.astype(jnp.float32)).astype(jnp.bfloat16)
        whole = lax.all_gather(sent, "team", axis=0, tiled=True)
        pieces = whole.reshape(col_blocks, block_size, width)

        def row_block(which, accum):

            def add_slot(slot, inner):
                tile = tiles[which, slot]
                piece = pieces[columns_used[which, slot]]
                return inner + jnp.dot(tile, piece, preferred_element_type=jnp.float32)

            block_rows = lax.fori_loop(
                0, counts_used[which], add_slot, jnp.zeros((block_size, width), jnp.float32)
            )
            return lax.dynamic_update_slice_in_dim(accum, block_rows, which * block_size, 0)

        partial_value = lax.fori_loop(
            0, row_blocks, row_block, jnp.zeros((panel, width), jnp.float32)
        )
        total = lax.psum_scatter(
            partial_value.astype(jnp.bfloat16), "rep", scatter_dimension=0, tiled=True
        ).astype(jnp.float32)
        current = (scale * (total + sent.astype(jnp.float32))).astype(jnp.bfloat16)
        results.append(current)
    return (results[0], results[1], results[2])


def solution(mesh):
    in_specs = (
        P(("team", "rep"), None),
        P(("team", "rep")),
        P("team", "rep", None, None, None),
        P("team", "rep", None),
        P("team", "rep"),
    )
    out_specs = (P(("team", "rep"), None), P(("team", "rep"), None), P(("team", "rep"), None))
    return jax.shard_map(
        on_device, mesh=mesh, in_specs=in_specs, out_specs=out_specs, check_vma=False
    )
```

profile of v0, /device:TPU:0, one launch (start us, length us, event | category | flops | bytes accessed | tf_op | source)
XLA Modules:
  0.0 128.9 jit_solution(8938508947645681261)
XLA Ops:
  7.2 0.0 reduce-scatter.4.cloned.1.call-start
  7.2 0.7 convert_rsqrt_fusion
  7.9 0.9 multiply_convert_fusion.5
  8.8 11.3 %all_gather.9 = bf16[256,1024]{1,0:T(8,128)(2,1)S(1)} all-gather(bf16[32,1024]{1,0:T(8,128)(2,1)S(1)} %multiply_convert_fusion.5), channel_id=1, replica_groups=mesh['team'=8,'rep'=4] {'team'}, dimensions={0}, use_global_device_ids=true | all-gather | bytes 589824 | tf_op jit(solution)/shard_map/all_gather | solution.py:23
  20.1 0.0 copy-start
  20.1 0.0 copy-start.4
  20.2 0.8 copy-done
  20.9 0.0 copy-done.4
  20.9 4.1 %while.57 = (s32[]{:T(128)}, f32[128,1024]{1,0:T(8,128)S(1)}, s32[]{:T(128)}, bf16[1,2,128,128]{3,2,1,0:T(8,128)(2,1)S(1)}, s32[1,2]{1,0:T(1,128)S(1)}, /*index=...) while((s32[]{:T(128)}, f32[128,1024]{1,0:T(8,128)S(1)}, s32[]{:T(128)}, ...), condition=%wide.region_1.2_spmd, body=%wide.region_0.1_spmd.sunk | while | flops 33685512 | bytes 1343677 | solution.py:33
  21.6 0.6 constant_dynamic-slice_fusion.6
  24.1 0.2 convolution_add_fusion.6
  25.0 0.7 convert_element_type.60
  25.8 0.0 copy-start.2
  25.8 0.0 reduce-scatter.4.cloned.1.call-update
  25.8 0.0 reduce-scatter.6.cloned.1.call-start
  25.9 22.4 %reduce-scatter.4.cloned.1.call-done = bf16[32,1024]{1,0:T(8,128)(2,1)} async-done(((bf16[128,1024]{1,0:T(8,128)(2,1)}), bf16[32,1024]{1,0:T(8,128)(2,1)}) %reduce-scatter.4.cloned.1.call-update) | async-done | bytes 65552 | tf_op jit(solution)/shard_map/reduce_scatter | solution.py:41
  48.3 0.0 copy-done.2
  48.3 0.9 multiply_convert_fusion.3
  49.2 0.0 copy-start.3
  49.2 9.9 %all_gather.10 = bf16[256,1024]{1,0:T(8,128)(2,1)S(1)} all-gather(bf16[32,1024]{1,0:T(8,128)(2,1)S(1)} %get-tuple-element.257), channel_id=1, replica_groups=mesh['team'=8,'rep'=4] {'team'}, dimensions={0}, use_global_device_ids=true | all-gather | bytes 589824 | tf_op jit(solution)/shard_map/all_gather | solution.py:23
  59.2 4.1 %while.58 = (s32[]{:T(128)}, f32[128,1024]{1,0:T(8,128)S(1)}, s32[]{:T(128)}, bf16[1,2,128,128]{3,2,1,0:T(8,128)(2,1)S(1)}, s32[1,2]{1,0:T(1,128)S(1)}, /*index=...) while((s32[]{:T(128)}, f32[128,1024]{1,0:T(8,128)S(1)}, s32[]{:T(128)}, ...), condition=%wide.region_4.0_spmd, body=%wide.region_3.0_spmd.sunk | while | flops 33685512 | bytes 1343677 | solution.py:33
  59.8 0.6 constant_dynamic-slice_fusion.7
  62.4 0.2 convolution_add_fusion.7
  63.3 0.7 convert_element_type.66
  64.0 0.0 reduce-scatter.6.cloned.1.call-update
  64.0 0.0 reduce-scatter.8.cloned.1.call-start
  64.1 20.4 %reduce-scatter.6.cloned.1.call-done = bf16[32,1024]{1,0:T(8,128)(2,1)} async-done(((bf16[128,1024]{1,0:T(8,128)(2,1)}), bf16[32,1024]{1,0:T(8,128)(2,1)}) %reduce-scatter.6.cloned.1.call-update) | async-done | bytes 65552 | tf_op jit(solution)/shard_map/reduce_scatter | solution.py:41
  84.5 0.0 copy-done.3
  84.5 0.9 multiply_convert_fusion.1
  85.5 0.0 copy-start.1
  85.5 9.9 %all_gather.11 = bf16[256,1024]{1,0:T(8,128)(2,1)S(1)} all-gather(bf16[32,1024]{1,0:T(8,128)(2,1)S(1)} %get-tuple-element.255), channel_id=1, replica_groups=mesh['team'=8,'rep'=4] {'team'}, dimensions={0}, use_global_device_ids=true | all-gather | bytes 589824 | tf_op jit(solution)/shard_map/all_gather | solution.py:23
  95.4 4.1 %while.59 = (s32[]{:T(128)}, f32[128,1024]{1,0:T(8,128)S(1)}, s32[]{:T(128)}, bf16[1,2,128,128]{3,2,1,0:T(8,128)(2,1)S(1)}, s32[1,2]{1,0:T(1,128)S(1)}, /*index=...) while((s32[]{:T(128)}, f32[128,1024]{1,0:T(8,128)S(1)}, s32[]{:T(128)}, ...), condition=%wide.region_7.8_spmd, body=%wide.region_6.7_spmd.sunk | while | flops 33685512 | bytes 1343677 | solution.py:33
  96.1 0.6 constant_dynamic-slice_fusion.8
  98.6 0.2 convolution_add_fusion.8
  99.5 0.7 convert_element_type.72
  100.3 0.0 reduce-scatter.8.cloned.1.call-update
  100.3 20.5 %reduce-scatter.8.cloned.1.call-done = bf16[32,1024]{1,0:T(8,128)(2,1)} async-done(((bf16[128,1024]{1,0:T(8,128)(2,1)}), bf16[32,1024]{1,0:T(8,128)(2,1)}) %reduce-scatter.8.cloned.1.call-update) | async-done | bytes 65552 | tf_op jit(solution)/shard_map/reduce_scatter | solution.py:41
  120.8 0.0 copy-done.1
  120.8 1.6 %multiply_convert_fusion = bf16[32,1024]{1,0:T(8,128)(2,1)} fusion(bf16[32,1024]{1,0:T(8,128)(2,1)} %reduce-scatter.8.cloned.1.call-done, f32[32]{0:T(128)S(1)} %convert_rsqrt_fusion, bf16[32,1024]{1,0:T(8,128)(2,1)S(1)} %get-tuple-element.256), kind=kLoop, calls=%fused_computation.21 | loop fusion | flops 262144 | bytes 196736 | tf_op jit(solution)/shard_map/convert_element_type | solution.py:44
  (3 shorter events, 0.1 us)
Async XLA Ops:
  7.2 41.1 %reduce-scatter.4.cloned.1.call-start = ((), (), s32[]{:S(2)}) async-start(), calls=%async_computation.3 | async-start | bytes 327680 | tf_op jit(solution)/shard_map/reduce_scatter | solution.py:41
  20.1 0.8 copy-start
  20.1 0.8 copy-start.4
  25.8 22.5 %copy-start.2 = (bf16[32,1024]{1,0:T(8,128)(2,1)S(1)}, bf16[32,1024]{1,0:T(8,128)(2,1)}, u32[]{:S(2)}) copy-start(bf16[32,1024]{1,0:T(8,128)(2,1)} %param.11) | copy-start | bytes 196612
  25.8 58.7 %reduce-scatter.6.cloned.1.call-start = ((), (), s32[]{:S(2)}) async-start(), calls=%async_computation.4 | async-start | bytes 327680 | tf_op jit(solution)/shard_map/reduce_scatter | solution.py:41
  49.2 35.3 %copy-start.3 = (bf16[32,1024]{1,0:T(8,128)(2,1)}, bf16[32,1024]{1,0:T(8,128)(2,1)S(1)}, u32[]{:S(2)}) copy-start(bf16[32,1024]{1,0:T(8,128)(2,1)S(1)} %get-tuple-element.258) | copy-start | bytes 196612
  64.0 56.8 %reduce-scatter.8.cloned.1.call-start = ((), (), s32[]{:S(2)}) async-start(), calls=%async_computation.5 | async-start | bytes 327680 | tf_op jit(solution)/shard_map/reduce_scatter | solution.py:41
  85.5 35.4 %copy-start.1 = (bf16[32,1024]{1,0:T(8,128)(2,1)}, bf16[32,1024]{1,0:T(8,128)(2,1)S(1)}, u32[]{:S(2)}) copy-start(bf16[32,1024]{1,0:T(8,128)(2,1)S(1)} %get-tuple-element.256) | copy-start | bytes 196612
Sparse Core Ops, SparseCore 0:
  25.9 22.2 reduce-scatter.3
  64.2 20.3 reduce-scatter.5
  100.4 20.3 reduce-scatter.7
where the time goes:
time: 130 us; the launch traced here: 129 us
  waiting for transfers between devices  63.4 us (49%)
  blocking collectives  31.1 us (24%)
  between operations  13.8 us (11%)
  loops' own time  9.76 us (8%)
  other arithmetic  7.25 us (6%)
  local copies, waits for them, and re-layouts  2.71 us (2%)
    reduce_scatter x3, waiting for transfers between devices, on_device(): lax.psum_scatter(partial_value.astype(jnp.bfloat16), 'rep', scatter_dimen...  63.4 us
    all_gather x3, blocking collectives, on_device(): whole = lax.all_gather(sent, 'team', axis=0, tiled=True)  31.1 us
    another operation x3, loops' own time, row_block(): lax.fori_loop(0, counts_used[which], add_slot, jnp.zeros((block_size, wid...  9.76 us
    convert_element_type x3, other arithmetic, on_device(): sent = (scale * current.astype(jnp.float32)).astype(jnp.bfloat16)  2.79 us
  transfers between devices with their start and end apart: 3, of which 3 were waited for; matrix products, arithmetic and copies ran while one was open for 0% of the time, Pallas kernels for 0%

commit v1 on v0

--- a/solution.py
+++ b/solution.py
@@ -1,12 +1,199 @@
+import functools
+
 import jax
 import jax.numpy as jnp
 from jax import lax
+from jax.experimental import pallas as pl
+from jax.experimental.pallas import tpu as pltpu
 from jax.sharding import PartitionSpec as P
 
 HOPS = 3
-
-
-def on_device(features, degree, blocks, block_cols, block_count):
+PAIR = 2
+LANES = 128
+MESH_IDS = pl.DeviceIdType.MESH
+
+
+def diffuse_kernel(n_team, n_rep, features, degree, blocks, block_cols, block_count,
+                   out1, out2, out3, sent, gathered, adjacency, scales, hops,
+                   feat_send, feat_recv, scale_send, scale_recv, adj_send, adj_recv,
+                   pass_send, pass_recv, hop_send, hop_recv, out_send, out_recv):
+    groups = n_rep * PAIR
+    chips = n_team // PAIR
+    rows, width = features.shape
+    group_width = width // groups
+    slots, block_size = blocks.shape[2], blocks.shape[-1]
+    panel = n_rep * rows
+    team, rep = lax.axis_index("team"), lax.axis_index("rep")
+    chip, core = team // PAIR, lax.rem(team, PAIR)
+    group = rep * PAIR + core
+    outs = (out1, out2, out3)
+
+    def column_peer(step):
+        other = lax.rem(group + step, groups)
+        return other, (chip * PAIR + lax.rem(other, PAIR), other // PAIR)
+
+    def plane_peer(step):
+        return (lax.rem(chip + step, chips) * PAIR + core, rep)
+
+    def remote(src, dst, send_sem, recv_sem, device):
+        return pltpu.make_async_remote_copy(
+            src_ref=src, dst_ref=dst, send_sem=send_sem, recv_sem=recv_sem,
+            device_id=device, device_id_type=MESH_IDS)
+
+    barrier = pltpu.get_barrier_semaphore()
+    for step in range(1, groups):
+        pl.semaphore_signal(barrier, inc=1, device_id=column_peer(step)[1], device_id_type=MESH_IDS)
+    for step in range(1, chips):
+        pl.semaphore_signal(barrier, inc=1, device_id=plane_peer(step), device_id_type=MESH_IDS)
+
+    own_scale = lax.rsqrt(degree[...].astype(jnp.float32))
+
+    def as_column(row):
+        on_diagonal = (lax.broadcasted_iota(jnp.int32, (rows, rows), 0)
+                       == lax.broadcasted_iota(jnp.int32, (rows, rows), 1))
+        spread = jnp.where(on_diagonal, jnp.broadcast_to(row, (rows, rows)), 0.0)
+        return jnp.sum(spread, axis=1, keepdims=True)
+
+    own_column = as_column(own_scale)
+    for index in range(groups):
+        part = features[:, index * group_width:(index + 1) * group_width].astype(jnp.float32)
+        sent[index] = (own_column * part).astype(jnp.bfloat16)
+    scales[core, rep, 0:1, 0:rows] = own_scale
+
+    for column in range(n_team * rows // block_size):
+        dense = jnp.zeros((block_size, block_size), jnp.float32)
+        for slot in range(slots):
+            used = (block_cols[0, 0, slot] == column) & (slot < block_count[0, 0])
+            factor = jnp.where(used, 1.0, 0.0).astype(jnp.float32)
+            dense = dense + factor * blocks[0, 0, slot].astype(jnp.float32)
+        adjacency[rep, core, :, column * block_size:(column + 1) * block_size] = dense.astype(jnp.bfloat16)
+
+    pl.semaphore_wait(barrier, groups - 1 + chips - 1)
+
+    feature_copies, scale_copies, adjacency_copies, pass_copies = [], [], [], []
+    for step in range(1, groups):
+        other, device = column_peer(step)
+        copy = remote(sent.at[other], gathered.at[0, rep, team],
+                      feat_send.at[step - 1], feat_recv.at[step - 1], device)
+        copy.start()
+        feature_copies.append(copy)
+    sibling = (chip * PAIR + lax.rem(core + 1, PAIR), rep)
+    copy = remote(adjacency.at[rep, core], adjacency.at[rep, core],
+                  pass_send.at[0], pass_recv.at[0], sibling)
+    copy.start()
+    pass_copies.append(copy)
+    for step in range(1, n_rep):
+        copy = remote(adjacency.at[rep, core], adjacency.at[rep, core],
+                      adj_send.at[step - 1], adj_recv.at[step - 1],
+                      (team, lax.rem(rep + step, n_rep)))
+        copy.start()
+        adjacency_copies.append(copy)
+    for step in range(1, groups):
+        copy = remote(scales.at[core, rep], scales.at[core, rep],
+                      scale_send.at[step - 1], scale_recv.at[step - 1], column_peer(step)[1])
+        copy.start()
+        scale_copies.append(copy)
+    gathered[0, rep, team] = sent[group]
+
+    def send_hop(hop):
+        copies = []
+        for step in range(1, chips):
+            own = gathered.at[hop, :, pl.ds(chip * PAIR, PAIR)]
+            copy = remote(own, own, hop_send.at[hop, step - 1], hop_recv.at[hop, step - 1],
+                          plane_peer(step))
+            copy.start()
+            copies.append(copy)
+        return copies
+
+    for copy in feature_copies:
+        copy.wait_recv()
+    hop_copies = [send_hop(0)]
+
+    for step in range(1, n_rep):
+        adjacency_copies[step - 1].wait_recv()
+        source = lax.rem(rep + n_rep - step, n_rep)
+        copy = remote(adjacency.at[source, core], adjacency.at[source, core],
+                      pass_send.at[step], pass_recv.at[step], sibling)
+        copy.start()
+        pass_copies.append(copy)
+    for copy in scale_copies:
+        copy.wait_recv()
+    scale_column = jnp.concatenate(
+        [as_column(scales[c, r, 0:1, 0:rows]) for c in range(PAIR) for r in range(n_rep)], axis=0)
+    for copy in pass_copies:
+        copy.wait_recv()
+
+    out_copies = []
+    for hop in range(HOPS):
+        for copy in hop_copies[hop]:
+            copy.wait_recv()
+        total = jnp.concatenate(
+            [gathered[hop, :, chip * PAIR + c].reshape(panel, group_width) for c in range(PAIR)],
+            axis=0).astype(jnp.float32)
+        for r in range(n_rep):
+            total = total + jnp.dot(
+                adjacency[r].reshape(PAIR * panel, n_team * rows),
+                gathered[hop, r].reshape(n_team * rows, group_width),
+                preferred_element_type=jnp.float32)
+        current = (scale_column * total).astype(jnp.bfloat16)
+        if hop < HOPS - 1:
+            following = (scale_column * current.astype(jnp.float32)).astype(jnp.bfloat16)
+            following = following.reshape(PAIR, n_rep, rows, group_width)
+            for c in range(PAIR):
+                gathered[hop + 1, :, chip * PAIR + c] = following[c]
+            hop_copies.append(send_hop(hop + 1))
+        hops[hop] = current.reshape(PAIR, n_rep, rows, group_width)
+        mine = pl.ds(pl.multiple_of(group * group_width, LANES), group_width)
+        for step in range(1, groups):
+            other, device = column_peer(step)
+            copy = remote(hops.at[hop, lax.rem(other, PAIR), other // PAIR],
+                          outs[hop].at[:, mine],
+                          out_send.at[hop, step - 1], out_recv.at[hop, step - 1], device)
+            copy.start()
+            out_copies.append(copy)
+        outs[hop][:, mine] = hops[hop, core, rep]
+
+    for copy in out_copies:
+        copy.wait_recv()
+    for copies in [feature_copies, scale_copies, adjacency_copies, pass_copies, out_copies] + hop_copies:
+        for copy in copies:
+            copy.wait_send()
+
+
+def exchange_columns(n_team, n_rep, features, degree, blocks, block_cols, block_count):
+    rows, width = features.shape
+    groups = n_rep * PAIR
+    chips = n_team // PAIR
+    group_width = width // groups
+    panel = n_rep * rows
+    dma = pltpu.SemaphoreType.DMA
+    vmem = pl.BlockSpec(memory_space=pltpu.VMEM)
+    smem = pl.BlockSpec(memory_space=pltpu.SMEM)
+    result = jax.ShapeDtypeStruct((rows, width), jnp.bfloat16)
+    return pl.pallas_call(
+        functools.partial(diffuse_kernel, n_team, n_rep),
+        out_shape=(result,) * HOPS,
+        in_specs=[vmem, vmem, vmem, smem, smem],
+        out_specs=(vmem,) * HOPS,
+        scratch_shapes=[
+            pltpu.VMEM((groups, rows, group_width), jnp.bfloat16),
+            pltpu.VMEM((HOPS, n_rep, n_team, rows, group_width), jnp.bfloat16),
+            pltpu.VMEM((n_rep, PAIR, panel, n_team * rows), jnp.bfloat16),
+            pltpu.VMEM((PAIR, n_rep, 8, LANES), jnp.float32),
+            pltpu.VMEM((HOPS, PAIR, n_rep, rows, group_width), jnp.bfloat16),
+            dma((groups - 1,)), dma((groups - 1,)),
+            dma((groups - 1,)), dma((groups - 1,)),
+            dma((n_rep - 1,)), dma((n_rep - 1,)),
+            dma((n_rep,)), dma((n_rep,)),
+            dma((HOPS, chips - 1)), dma((HOPS, chips - 1)),
+            dma((HOPS, groups - 1)), dma((HOPS, groups - 1)),
+        ],
+        compiler_params=pltpu.CompilerParams(
+            collective_id=0, has_side_effects=True, vmem_limit_bytes=24 * 1024 * 1024),
+    )(features, degree[None, :], blocks, block_cols, block_count)
+
+
+def gather_and_scatter(features, degree, blocks, block_cols, block_count):
     width = features.shape[1]
     block_size = blocks.shape[-1]
     row_blocks = blocks.shape[0]
@@ -46,7 +233,24 @@
     return (results[0], results[1], results[2])
 
 
+def fits_columns(n_team, n_rep, features, blocks):
+    rows, width = features.shape
+    return (width % (n_rep * PAIR * LANES) == 0 and n_team % PAIR == 0 and n_team > PAIR
+            and n_rep > 1 and blocks.shape[0] == 1 and rows % 16 == 0 and rows <= LANES
+            and blocks.shape[-1] == n_rep * rows
+            and blocks.shape[-1] % LANES == 0
+            and n_rep * n_team * rows * n_rep * rows * 4 <= 4 * 1024 * 1024)
+
+
 def solution(mesh):
+    n_team, n_rep = mesh.shape["team"], mesh.shape["rep"]
+
+    def on_device(features, degree, blocks, block_cols, block_count):
+        arrays = (features, degree, blocks, block_cols, block_count)
+        if fits_columns(n_team, n_rep, features, blocks):
+            return exchange_columns(n_team, n_rep, *arrays)
+        return gather_and_scatter(*arrays)
+
     in_specs = (
         P(("team", "rep"), None),
         P(("team", "rep")),

time: 130 us -> 37.5 us (0.29)
  waiting for transfers between devices: 63.4 us -> 0 us
  Pallas kernels: 0 us -> 31.8 us
  blocking collectives: 31.1 us -> 0 us
  between operations: 13.8 us -> 1.31 us
  loops' own time: 9.76 us -> 0 us
  other arithmetic: 7.25 us -> 0 us
  local copies, waits for them, and re-layouts: 2.71 us -> 4.22 us
    reduce_scatter x3 -> x0, waiting for transfers between devices: 63.4 us -> none  [on_device(): lax.psum_scatter(partial_value.astype(jnp.bfloat16), 'rep', scatter_dimen...]
    pallas_call x0 -> x1, Pallas kernels: none -> 31.8 us  [exchange_columns(): pl.pallas_call(functools.partial(diffuse_kernel, n_team, n_rep), out_shap...]
    all_gather x3 -> x0, blocking collectives: 31.1 us -> none  [on_device(): whole = lax.all_gather(sent, 'team', axis=0, tiled=True)]
    another operation x3 -> x0, loops' own time: 9.76 us -> none  [row_block(): lax.fori_loop(0, counts_used[which], add_slot, jnp.zeros((block_size, wid...]
    convert_element_type x7 -> x0, other arithmetic: 6.59 us -> none  [the longest x3 2.79 us: on_device(): sent = (scale * current.astype(jnp.float32)).astype(jnp.bfloat16)]
    unnamed x10 -> x11, local copies, waits for them, and re-layouts: 0.81 us -> 4.22 us
    dynamic_slice x3 -> x0, local copies, waits for them, and re-layouts: 1.78 us -> none  [add_slot(): piece = pieces[columns_used[which, slot]]]
  transfers between devices with their start and end apart: 3 -> 0, of which waited for: 3 -> 0; matrix products, arithmetic and copies ran while one was open for 0% -> 0% of each run, Pallas kernels for 0% -> 0%
where the time goes in v1:
time: 37.5 us; the launch traced here: 37.3 us
  Pallas kernels  31.8 us (85%)
  local copies, waits for them, and re-layouts  4.22 us (11%)
  between operations  1.31 us (3%)
    pallas_call x1, Pallas kernels, exchange_columns(): pl.pallas_call(functools.partial(diffuse_kernel, n_team, n_rep), out_shap...  31.8 us
    unnamed x11, local copies, waits for them, and re-layouts  4.22 us

profile of v1, /device:TPU:0, one launch (start us, length us, event | category | flops | bytes accessed | tf_op | source)
XLA Modules:
  0.0 37.3 jit_solution(2299649298209725308)
XLA Ops:
  1.3 0.0 copy-start.2
  1.3 0.0 copy-start.3
  1.3 0.6 %copy-done.2 = s32[32]{0:T(128)S(1)} copy-done((s32[32]{0:T(128)S(1)}, s32[32]{0:T(128)}, u32[]{:S(2)}) %copy-start.2) | copy-done | bytes 152
  1.9 0.0 copy-done.3
  1.9 0.0 copy-start
  2.0 0.8 %copy-done = bf16[32,1024]{1,0:T(8,128)(2,1)S(1)} copy-done((bf16[32,1024]{1,0:T(8,128)(2,1)S(1)}, bf16[32,1024]{1,0:T(8,128)(2,1)}, u32[]{:S(2)}) %copy-start) | copy-done | bytes 65560
  2.8 0.0 copy-start.1
  2.8 0.8 %copy-done.1 = bf16[1,1,2,128,128]{4,3,2,1,0:T(8,128)(2,1)S(1)} copy-done((bf16[1,1,2,128,128]{4,3,2,1,0:T(8,128)(2,1)S(1)}, bf16[1,1,2,128,128]{4,3,2,1,0:T(8,128)(2,1)}, u32[]{:S(2)}) %copy-start.1) | copy-done | bytes 65560
  3.6 31.8 %shard_map.76 = (bf16[32,1024]{1,0:T(8,128)(2,1)S(1)}, bf16[32,1024]{1,0:T(8,128)(2,1)S(1)}, bf16[32,1024]{1,0:T(8,128)(2,1)S(1)}) custom-call(bf16[32,1024]{1,0:T(8,128)(2,1)S(1)} %copy-done, s32[1,32]{1,0:T(1,128)S(1)} %bitcast.1, bf16[1,1,2,128,128]{4,3,2,1,0:T(8,128)(2,1)S(1)} %copy-done.1, s32[1,1,2]{2,1,0:T(1,128)S(1)} %copy-done.3, ...), custom_call_target="tpu_custom_call" | custom-call | tf_op jit(solution)/shard_map/pallas_call | solution.py:173
  35.4 0.6 %copy.12 = bf16[32,1024]{1,0:T(8,128)(2,1)} copy(bf16[32,1024]{1,0:T(8,128)(2,1)S(1)} %get-tuple-element.6) | data formatting | bytes 131072
  36.0 0.6 %copy.13 = bf16[32,1024]{1,0:T(8,128)(2,1)} copy(bf16[32,1024]{1,0:T(8,128)(2,1)S(1)} %get-tuple-element.7) | data formatting | bytes 131072
  36.7 0.6 %copy.14 = bf16[32,1024]{1,0:T(8,128)(2,1)} copy(bf16[32,1024]{1,0:T(8,128)(2,1)S(1)} %get-tuple-element.8) | data formatting | bytes 131072
Async XLA Ops:
  1.3 0.7 %copy-start.2 = (s32[32]{0:T(128)S(1)}, s32[32]{0:T(128)}, u32[]{:S(2)}) copy-start(s32[32]{0:T(128)} %param.6) | copy-start | bytes 388
  1.3 0.7 %copy-start.3 = (s32[1,1,2]{2,1,0:T(1,128)S(1)}, s32[1,1,2]{2,1,0:T(1,128)}, u32[]{:S(2)}) copy-start(s32[1,1,2]{2,1,0:T(1,128)} %block_cols.1) | copy-start | bytes 28
  1.9 0.8 %copy-start = (bf16[32,1024]{1,0:T(8,128)(2,1)S(1)}, bf16[32,1024]{1,0:T(8,128)(2,1)}, u32[]{:S(2)}) copy-start(bf16[32,1024]{1,0:T(8,128)(2,1)} %features.1) | copy-start | bytes 196612
  2.8 0.8 %copy-start.1 = (bf16[1,1,2,128,128]{4,3,2,1,0:T(8,128)(2,1)S(1)}, bf16[1,1,2,128,128]{4,3,2,1,0:T(8,128)(2,1)}, u32[]{:S(2)}) copy-start(bf16[1,1,2,128,128]{4,3,2,1,0:T(8,128)(2,1)} %blocks.1) | copy-start | bytes 196612

commit v2 on v1

v2 whole, which is shorter than its diff:
```python
import functools

import jax
import jax.numpy as jnp
from jax import lax
from jax.experimental import pallas as pl
from jax.experimental.pallas import tpu as pltpu
from jax.sharding import PartitionSpec as P

HOPS = 3
PAIR = 2
LANES = 128
MESH_IDS = pl.DeviceIdType.MESH


def diffuse_kernel(n_team, n_rep, features_in, degree_in, blocks_in, cols_in, count_in,
                   out1, out2, out3, features, degree, blocks, block_cols, block_count,
                   sent, gathered, adjacency, scales, hops, in_sem,
                   feat_send, feat_recv, scale_send, scale_recv, adj_send, adj_recv,
                   pass_send, pass_recv, hop_send, hop_recv, out_send, out_recv, keep_sem):
    groups = n_rep * PAIR
    chips = n_team // PAIR
    rows, width = features.shape
    group_width = width // groups
    slots, block_size = blocks.shape[2], blocks.shape[-1]
    panel = n_rep * rows
    col_blocks = n_team * rows // block_size
    team_run = n_team // col_blocks
    team, rep = lax.axis_index("team"), lax.axis_index("rep")
    chip, core = team // PAIR, lax.rem(team, PAIR)
    group = rep * PAIR + core
    outs = (out1, out2, out3)

    loads = []
    for index, (src, dst) in enumerate(((features_in, features), (degree_in, degree),
                                        (blocks_in, blocks), (cols_in, block_cols),
                                        (count_in, block_count))):
        copy = pltpu.make_async_copy(src, dst, in_sem.at[index])
        copy.start()
        loads.append(copy)

    def column_peer(step):
        other = lax.rem(group + step, groups)
        return other, (chip * PAIR + lax.rem(other, PAIR), other // PAIR)

    def plane_peer(step):
        other = (chip + 1 - 2 * lax.rem(chip, 2), lax.rem(chip + 2, chips), chips - 1 - chip)[step - 1]
        return (other * PAIR + core, rep)

    def remote(src, dst, send_sem, recv_sem, device):
        return pltpu.make_async_remote_copy(
            src_ref=src, dst_ref=dst, send_sem=send_sem, recv_sem=recv_sem,
            device_id=device, device_id_type=MESH_IDS)

    barrier = pltpu.get_barrier_semaphore()
    for step in range(1, groups):
        pl.semaphore_signal(barrier, inc=1, device_id=column_peer(step)[1], device_id_type=MESH_IDS)
    for step in range(1, chips):
        pl.semaphore_signal(barrier, inc=1, device_id=plane_peer(step), device_id_type=MESH_IDS)

    for copy in loads:
        copy.wait()
    own_scale = lax.rsqrt(degree[...].astype(jnp.float32))

    def as_column(row):
        on_diagonal = (lax.broadcasted_iota(jnp.int32, (rows, rows), 0)
                       == lax.broadcasted_iota(jnp.int32, (rows, rows), 1))
        spread = jnp.where(on_diagonal, jnp.broadcast_to(row, (rows, rows)), 0.0)
        return jnp.sum(spread, axis=1, keepdims=True)

    own_column = as_column(own_scale)
    for index in range(groups):
        part = features[:, index * group_width:(index + 1) * group_width].astype(jnp.float32)
        sent[index] = (own_column * part).astype(jnp.bfloat16)
    scales[core, rep, 0:1, 0:rows] = own_scale

    def replica_columns(which):
        return pl.ds(pl.multiple_of(which * block_size, LANES), block_size)

    for column in range(col_blocks):
        dense = jnp.zeros((block_size, block_size), jnp.float32)
        for slot in range(slots):
            used = (block_cols[0, 0, slot] == column) & (slot < block_count[0, 0])
            factor = jnp.where(used, 1.0, 0.0).astype(jnp.float32)
            dense = dense + factor * blocks[0, 0, slot].astype(jnp.float32)
        adjacency[column, core, :, replica_columns(rep)] = dense.astype(jnp.bfloat16)

    pl.semaphore_wait(barrier, groups - 1 + chips - 1)

    feature_copies, scale_copies, adjacency_copies, pass_copies = [], [], [], []
    for step in range(1, groups):
        other, device = column_peer(step)
        copy = remote(sent.at[other], gathered.at[0, rep, team],
                      feat_send.at[step - 1], feat_recv.at[step - 1], device)
        copy.start()
        feature_copies.append(copy)

    def adjacency_of(which):
        return adjacency.at[:, core, :, replica_columns(which)]

    sibling = (chip * PAIR + lax.rem(core + 1, PAIR), rep)
    for step in range(1, n_rep):
        copy = remote(adjacency_of(rep), adjacency_of(rep),
                      adj_send.at[step - 1], adj_recv.at[step - 1],
                      (team, lax.rem(rep + step, n_rep)))
        copy.start()
        adjacency_copies.append(copy)
    copy = remote(adjacency_of(rep), adjacency_of(rep), pass_send.at[0], pass_recv.at[0], sibling)
    copy.start()
    pass_copies.append(copy)
    for step in range(1, groups):
        copy = remote(scales.at[core, rep], scales.at[core, rep],
                      scale_send.at[step - 1], scale_recv.at[step - 1], column_peer(step)[1])
        copy.start()
        scale_copies.append(copy)
    gathered[0, rep, team] = sent[group]

    panels = (lax.rem(core + 1, PAIR), core)

    def send_hop(hop, half):
        copies = []
        own = gathered.at[hop, :, chip * PAIR + panels[half]]
        for step in (1, 3, 2):
            copy = remote(own, own, hop_send.at[hop, half, step - 1],
                          hop_recv.at[hop, half, step - 1], plane_peer(step))
            copy.start()
            copies.append(copy)
        return copies

    for copy in feature_copies:
        copy.wait_recv()
    hop_copies = [[send_hop(0, half) for half in range(PAIR)]]

    for step in range(1, n_rep):
        adjacency_copies[step - 1].wait_recv()
        source = lax.rem(rep + n_rep - step, n_rep)
        copy = remote(adjacency_of(source), adjacency_of(source),
                      pass_send.at[step], pass_recv.at[step], sibling)
        copy.start()
        pass_copies.append(copy)
    for copy in scale_copies:
        copy.wait_recv()
    scale_columns = [
        jnp.concatenate([as_column(scales[c, r, 0:1, 0:rows]) for r in range(n_rep)], axis=0)
        for c in panels]
    for copy in pass_copies:
        copy.wait_recv()

    near = team // team_run
    mine = pl.ds(pl.multiple_of(group * group_width, LANES), group_width)

    def product(hop, column, c):
        piece = gathered[hop, :, pl.ds(column * team_run, team_run)]
        return jnp.dot(adjacency[column, c], piece.reshape(n_rep * block_size, group_width),
                       preferred_element_type=jnp.float32)

    out_copies, kept_copies = [], []
    for hop in range(HOPS):
        for copies in hop_copies[hop]:
            copies[0].wait_recv()
        totals = []
        for c in panels:
            own = gathered[hop, :, chip * PAIR + c].reshape(panel, group_width)
            totals.append(own.astype(jnp.float32) + product(hop, near, c))
        for copies in hop_copies[hop]:
            for copy in copies[1:]:
                copy.wait_recv()
        if hop < HOPS - 1:
            hop_copies.append([])
        for half, c in enumerate(panels):
            total = totals[half] + product(hop, col_blocks - 1 - near, c)
            current = (scale_columns[half] * total).astype(jnp.bfloat16)
            if hop < HOPS - 1:
                following = (scale_columns[half] * current.astype(jnp.float32)).astype(jnp.bfloat16)
                gathered[hop + 1, :, chip * PAIR + c] = following.reshape(n_rep, rows, group_width)
                hop_copies[hop + 1].append(send_hop(hop + 1, half))
            hops[hop, c] = current.reshape(n_rep, rows, group_width)
            for step in range(1, groups):
                if step % PAIR == 1 - half:
                    other, device = column_peer(step)
                    copy = remote(hops.at[hop, c, other // PAIR], outs[hop].at[:, mine],
                                  out_send.at[hop, step - 1], out_recv.at[hop, step - 1], device)
                    copy.start()
                    out_copies.append(copy)
        kept = pltpu.make_async_copy(hops.at[hop, core, rep], outs[hop].at[:, mine], keep_sem.at[hop])
        kept.start()
        kept_copies.append(kept)

    for copy in out_copies:
        copy.wait_recv()
    for copy in kept_copies:
        copy.wait()
    for copies in [feature_copies, scale_copies, adjacency_copies, pass_copies, out_copies]:
        for copy in copies:
            copy.wait_send()
    for halves in hop_copies:
        for copies in halves:
            for copy in copies:
                copy.wait_send()


def store_kernel(in1, in2, in3, out1, out2, out3, sem):
    copies = [pltpu.make_async_copy(src, dst, sem.at[index])
              for index, (src, dst) in enumerate(((in1, out1), (in2, out2), (in3, out3)))]
    for copy in copies:
        copy.start()
    for copy in copies:
        copy.wait()


def exchange_columns(n_team, n_rep, features, degree, blocks, block_cols, block_count):
    rows, width = features.shape
    groups = n_rep * PAIR
    chips = n_team // PAIR
    group_width = width // groups
    panel = n_rep * rows
    col_blocks = n_team * rows // panel
    dma = pltpu.SemaphoreType.DMA
    hbm = pl.BlockSpec(memory_space=pltpu.HBM)
    result = jax.ShapeDtypeStruct((rows, width), jnp.bfloat16)
    results = pl.pallas_call(
        functools.partial(diffuse_kernel, n_team, n_rep),
        out_shape=(result,) * HOPS,
        in_specs=[hbm] * 5,
        out_specs=(hbm,) * HOPS,
        scratch_shapes=[
            pltpu.VMEM((rows, width), jnp.bfloat16),
            pltpu.VMEM((1, rows), jnp.int32),
            pltpu.VMEM(blocks.shape, jnp.bfloat16),
            pltpu.SMEM(block_cols.shape, jnp.int32),
            pltpu.SMEM(block_count.shape, jnp.int32),
            pltpu.VMEM((groups, rows, group_width), jnp.bfloat16),
            pltpu.VMEM((HOPS, n_rep, n_team, rows, group_width), jnp.bfloat16),
            pltpu.VMEM((col_blocks, PAIR, panel, n_rep * panel), jnp.bfloat16),
            pltpu.VMEM((PAIR, n_rep, 8, LANES), jnp.float32),
            pltpu.VMEM((HOPS, PAIR, n_rep, rows, group_width), jnp.bfloat16),
            dma((5,)),
            dma((groups - 1,)), dma((groups - 1,)),
            dma((groups - 1,)), dma((groups - 1,)),
            dma((n_rep - 1,)), dma((n_rep - 1,)),
            dma((n_rep,)), dma((n_rep,)),
            dma((HOPS, PAIR, chips - 1)), dma((HOPS, PAIR, chips - 1)),
            dma((HOPS, groups - 1)), dma((HOPS, groups - 1)),
            dma((HOPS,)),
        ],
        compiler_params=pltpu.CompilerParams(
            collective_id=0, has_side_effects=True, vmem_limit_bytes=62 * 1024 * 1024),
    )(features, degree[None, :], blocks, block_cols, block_count)
    return pl.pallas_call(
        store_kernel,
        out_shape=(result,) * HOPS,
        in_specs=[hbm] * HOPS,
        out_specs=(hbm,) * HOPS,
        scratch_shapes=[dma((HOPS,))],
        compiler_params=pltpu.CompilerParams(vmem_limit_bytes=62 * 1024 * 1024),
    )(*results)


def gather_and_scatter(features, degree, blocks, block_cols, block_count):
    width = features.shape[1]
    block_size = blocks.shape[-1]
    row_blocks = blocks.shape[0]
    col_blocks = blocks.shape[2]
    panel = row_blocks * block_size
    tiles = blocks[:, 0]
    columns_used = block_cols[:, 0]
    counts_used = block_count[:, 0]
    scale = lax.rsqrt(degree.astype(jnp.float32))[:, None]
    current = features
    results = []
    for hop in range(HOPS):
        sent = (scale * current.astype(jnp.float32)).astype(jnp.bfloat16)
        whole = lax.all_gather(sent, "team", axis=0, tiled=True)
        pieces = whole.reshape(col_blocks, block_size, width)

        def row_block(which, accum):

            def add_slot(slot, inner):
                tile = tiles[which, slot]
                piece = pieces[columns_used[which, slot]]
                return inner + jnp.dot(tile, piece, preferred_element_type=jnp.float32)

            block_rows = lax.fori_loop(
                0, counts_used[which], add_slot, jnp.zeros((block_size, width), jnp.float32)
            )
            return lax.dynamic_update_slice_in_dim(accum, block_rows, which * block_size, 0)

        partial_value = lax.fori_loop(
            0, row_blocks, row_block, jnp.zeros((panel, width), jnp.float32)
        )
        total = lax.psum_scatter(
            partial_value.astype(jnp.bfloat16), "rep", scatter_dimension=0, tiled=True
        ).astype(jnp.float32)
        current = (scale * (total + sent.astype(jnp.float32))).astype(jnp.bfloat16)
        results.append(current)
    return (results[0], results[1], results[2])


def fits_columns(n_team, n_rep, features, blocks):
    rows, width = features.shape
    return (width % (n_rep * PAIR * LANES) == 0 and n_team == 4 * PAIR
            and n_team * rows == 2 * blocks.shape[-1]
            and n_rep > 1 and blocks.shape[0] == 1 and rows % 16 == 0 and rows <= LANES
            and blocks.shape[-1] == n_rep * rows
            and blocks.shape[-1] % LANES == 0
            and n_rep * n_team * rows * n_rep * rows * 4 <= 4 * 1024 * 1024)


def solution(mesh):
    n_team, n_rep = mesh.shape["team"], mesh.shape["rep"]

    def on_device(features, degree, blocks, block_cols, block_count):
        arrays = (features, degree, blocks, block_cols, block_count)
        if fits_columns(n_team, n_rep, features, blocks):
            return exchange_columns(n_team, n_rep, *arrays)
        return gather_and_scatter(*arrays)

    in_specs = (
        P(("team", "rep"), None),
        P(("team", "rep")),
        P("team", "rep", None, None, None),
        P("team", "rep", None),
        P("team", "rep"),
    )
    out_specs = (P(("team", "rep"), None), P(("team", "rep"), None), P(("team", "rep"), None))
    return jax.shard_map(
        on_device, mesh=mesh, in_specs=in_specs, out_specs=out_specs, check_vma=False
    )
```

time: 37.5 us -> 40.9 us (1.091)
  Pallas kernels: 31.8 us -> 39.4 us
  local copies, waits for them, and re-layouts: 4.22 us -> 0 us
    pallas_call x0 -> x1, Pallas kernels: none -> 7.09 us  [exchange_columns(): pl.pallas_call(store_kernel, out_shape=(result,) * HOPS, in_specs=[hbm] *...]
    unnamed x11 -> x0, local copies, waits for them, and re-layouts: 4.22 us -> none
    pallas_call x1, Pallas kernels: 31.8 us -> 32.3 us  [exchange_columns(): pl.pallas_call(functools.partial(diffuse_kernel, n_team, n_rep), out_shap...]
where the time goes in v2:
time: 40.9 us; the launch traced here: 40.7 us
  Pallas kernels  39.4 us (96%)
  between operations  1.29 us (3%)
    pallas_call x1, Pallas kernels, exchange_columns(): pl.pallas_call(functools.partial(diffuse_kernel, n_team, n_rep), out_shap...  32.3 us
    pallas_call x1, Pallas kernels, exchange_columns(): pl.pallas_call(store_kernel, out_shape=(result,) * HOPS, in_specs=[hbm] *...  7.09 us

profile of v2, /device:TPU:0, one launch (start us, length us, event | category | flops | bytes accessed | tf_op | source)
XLA Modules:
  0.0 40.7 jit_solution(15573587707353650963)
XLA Ops:
  1.3 32.3 %shard_map.76 = (bf16[32,1024]{1,0:T(8,128)(2,1)}, bf16[32,1024]{1,0:T(8,128)(2,1)}, bf16[32,1024]{1,0:T(8,128)(2,1)}) custom-call(bf16[32,1024]{1,0:T(8,128)(2,1)} %features_in.1, s32[1,32]{1,0:T(1,128)} %bitcast.1, bf16[1,1,2,128,128]{4,3,2,1,0:T(8,128)(2,1)} %blocks_in.1, s32[1,1,2]{2,1,0:T(1,128)} %cols_in.1, s32[1,1]{1,0:T(1,128)S(6)} %copy.8.count_in), custom_call_target="tpu_custom_call" | custom-call | tf_op jit(solution)/shard_map/pallas_call | solution.py:221
  33.6 7.1 %shard_map.77 = (bf16[32,1024]{1,0:T(8,128)(2,1)}, bf16[32,1024]{1,0:T(8,128)(2,1)}, bf16[32,1024]{1,0:T(8,128)(2,1)}) custom-call(bf16[32,1024]{1,0:T(8,128)(2,1)} %get-tuple-element.6.in1, bf16[32,1024]{1,0:T(8,128)(2,1)} %get-tuple-element.7.in2, bf16[32,1024]{1,0:T(8,128)(2,1)} %get-tuple-element.8.in3), custom_call_target="tpu_custom_call" | custom-call | tf_op jit(solution)/shard_map/pallas_call | solution.py:249

commit v3 on v2

--- a/solution.py
+++ b/solution.py
@@ -74,16 +74,13 @@
         sent[index] = (own_column * part).astype(jnp.bfloat16)
     scales[core, rep, 0:1, 0:rows] = own_scale
 
-    def replica_columns(which):
-        return pl.ds(pl.multiple_of(which * block_size, LANES), block_size)
-
     for column in range(col_blocks):
         dense = jnp.zeros((block_size, block_size), jnp.float32)
         for slot in range(slots):
             used = (block_cols[0, 0, slot] == column) & (slot < block_count[0, 0])
             factor = jnp.where(used, 1.0, 0.0).astype(jnp.float32)
             dense = dense + factor * blocks[0, 0, slot].astype(jnp.float32)
-        adjacency[column, core, :, replica_columns(rep)] = dense.astype(jnp.bfloat16)
+        adjacency[rep, core, column] = dense.astype(jnp.bfloat16)
 
     pl.semaphore_wait(barrier, groups - 1 + chips - 1)
 
@@ -96,7 +93,7 @@
         feature_copies.append(copy)
 
     def adjacency_of(which):
-        return adjacency.at[:, core, :, replica_columns(which)]
+        return adjacency.at[which, core]
 
     sibling = (chip * PAIR + lax.rem(core + 1, PAIR), rep)
     for step in range(1, n_rep):
@@ -143,32 +140,47 @@
     scale_columns = [
         jnp.concatenate([as_column(scales[c, r, 0:1, 0:rows]) for r in range(n_rep)], axis=0)
         for c in panels]
-    for copy in pass_copies:
-        copy.wait_recv()
 
     near = team // team_run
     mine = pl.ds(pl.multiple_of(group * group_width, LANES), group_width)
 
     def product(hop, column, c):
         piece = gathered[hop, :, pl.ds(column * team_run, team_run)]
-        return jnp.dot(adjacency[column, c], piece.reshape(n_rep * block_size, group_width),
+        weights = jnp.concatenate([adjacency[r, c, column] for r in range(n_rep)], axis=1)
+        return jnp.dot(weights, piece.reshape(n_rep * block_size, group_width),
                        preferred_element_type=jnp.float32)
 
     out_copies, kept_copies = [], []
     for hop in range(HOPS):
         for copies in hop_copies[hop]:
             copies[0].wait_recv()
-        totals = []
-        for c in panels:
-            own = gathered[hop, :, chip * PAIR + c].reshape(panel, group_width)
-            totals.append(own.astype(jnp.float32) + product(hop, near, c))
-        for copies in hop_copies[hop]:
-            for copy in copies[1:]:
-                copy.wait_recv()
+        totals = [gathered[hop, :, chip * PAIR + c].reshape(panel, group_width).astype(jnp.float32)
+                  for c in panels]
+        if hop == 0:
+            for copies in hop_copies[hop]:
+                for copy in copies[1:]:
+                    copy.wait_recv()
+            for step in range(n_rep):
+                pass_copies[step].wait_recv()
+                source = lax.rem(rep + n_rep - step, n_rep)
+                piece = gathered[hop, source].reshape(col_blocks * block_size, group_width)
+                for half, c in enumerate(panels):
+                    weights = jnp.concatenate(
+                        [adjacency[source, c, column] for column in range(col_blocks)], axis=1)
+                    totals[half] = totals[half] + jnp.dot(
+                        weights, piece, preferred_element_type=jnp.float32)
+        else:
+            for half, c in enumerate(panels):
+                totals[half] = totals[half] + product(hop, near, c)
+            for copies in hop_copies[hop]:
+                for copy in copies[1:]:
+                    copy.wait_recv()
         if hop < HOPS - 1:
             hop_copies.append([])
         for half, c in enumerate(panels):
-            total = totals[half] + product(hop, col_blocks - 1 - near, c)
+            total = totals[half]
+            if hop > 0:
+                total = total + product(hop, col_blocks - 1 - near, c)
             current = (scale_columns[half] * total).astype(jnp.bfloat16)
             if hop < HOPS - 1:
                 following = (scale_columns[half] * current.astype(jnp.float32)).astype(jnp.bfloat16)
@@ -199,13 +211,19 @@
                 copy.wait_send()
 
 
-def store_kernel(in1, in2, in3, out1, out2, out3, sem):
-    copies = [pltpu.make_async_copy(src, dst, sem.at[index])
-              for index, (src, dst) in enumerate(((in1, out1), (in2, out2), (in3, out3)))]
-    for copy in copies:
-        copy.start()
-    for copy in copies:
-        copy.wait()
+def store_kernel(in1, in2, in3, out1, out2, out3, held, load_sem, store_sem):
+    refs = ((in1, out1), (in2, out2), (in3, out3))
+    loads = [pltpu.make_async_copy(src, held.at[index], load_sem.at[index])
+             for index, (src, dst) in enumerate(refs)]
+    stores = [pltpu.make_async_copy(held.at[index], dst, store_sem.at[index])
+              for index, (src, dst) in enumerate(refs)]
+    for load in loads:
+        load.start()
+    for load, store in zip(loads, stores):
+        load.wait()
+        store.start()
+    for store in stores:
+        store.wait()
 
 
 def exchange_columns(n_team, n_rep, features, degree, blocks, block_cols, block_count):
@@ -231,7 +249,7 @@
             pltpu.SMEM(block_count.shape, jnp.int32),
             pltpu.VMEM((groups, rows, group_width), jnp.bfloat16),
             pltpu.VMEM((HOPS, n_rep, n_team, rows, group_width), jnp.bfloat16),
-            pltpu.VMEM((col_blocks, PAIR, panel, n_rep * panel), jnp.bfloat16),
+            pltpu.VMEM((n_rep, PAIR, col_blocks, panel, panel), jnp.bfloat16),
             pltpu.VMEM((PAIR, n_rep, 8, LANES), jnp.float32),
             pltpu.VMEM((HOPS, PAIR, n_rep, rows, group_width), jnp.bfloat16),
             dma((5,)),
@@ -251,7 +269,7 @@
         out_shape=(result,) * HOPS,
         in_specs=[hbm] * HOPS,
         out_specs=(hbm,) * HOPS,
-        scratch_shapes=[dma((HOPS,))],
+        scratch_shapes=[pltpu.VMEM((HOPS, rows, width), jnp.bfloat16), dma((HOPS,)), dma((HOPS,))],
         compiler_params=pltpu.CompilerParams(vmem_limit_bytes=62 * 1024 * 1024),
     )(*results)
 

time: 40.9 us -> 35.3 us (0.86)
  Pallas kernels: 39.4 us -> 33.7 us
    pallas_call x1, Pallas kernels: 7.09 us -> 1.58 us  [exchange_columns(): pl.pallas_call(store_kernel, out_shape=(result,) * HOPS, in_specs=[hbm] *...]
where the time goes in v3:
time: 35.3 us; the launch traced here: 35 us
  Pallas kernels  33.7 us (95%)
  between operations  1.29 us (4%)
    pallas_call x1, Pallas kernels, exchange_columns(): pl.pallas_call(functools.partial(diffuse_kernel, n_team, n_rep), out_shap...  32.2 us
    pallas_call x1, Pallas kernels, exchange_columns(): pl.pallas_call(store_kernel, out_shape=(result,) * HOPS, in_specs=[hbm] *...  1.58 us

profile of v3, /device:TPU:0, one launch (start us, length us, event | category | flops | bytes accessed | tf_op | source)
XLA Modules:
  0.0 35.0 jit_solution(266157028288487997)
XLA Ops:
  1.3 32.2 %shard_map.76 = (bf16[32,1024]{1,0:T(8,128)(2,1)}, bf16[32,1024]{1,0:T(8,128)(2,1)}, bf16[32,1024]{1,0:T(8,128)(2,1)}) custom-call(bf16[32,1024]{1,0:T(8,128)(2,1)} %features_in.1, s32[1,32]{1,0:T(1,128)} %bitcast.1, bf16[1,1,2,128,128]{4,3,2,1,0:T(8,128)(2,1)} %blocks_in.1, s32[1,1,2]{2,1,0:T(1,128)} %cols_in.1, s32[1,1]{1,0:T(1,128)S(6)} %copy.8.count_in), custom_call_target="tpu_custom_call" | custom-call | tf_op jit(solution)/shard_map/pallas_call | solution.py:239
  33.4 1.6 %shard_map.77 = (bf16[32,1024]{1,0:T(8,128)(2,1)}, bf16[32,1024]{1,0:T(8,128)(2,1)}, bf16[32,1024]{1,0:T(8,128)(2,1)}) custom-call(bf16[32,1024]{1,0:T(8,128)(2,1)} %get-tuple-element.6.in1, bf16[32,1024]{1,0:T(8,128)(2,1)} %get-tuple-element.7.in2, bf16[32,1024]{1,0:T(8,128)(2,1)} %get-tuple-element.8.in3), custom_call_target="tpu_custom_call" | custom-call | tf_op jit(solution)/shard_map/pallas_call | solution.py:267

commit v4 on v3

--- a/solution.py
+++ b/solution.py
@@ -14,9 +14,9 @@
 
 
 def diffuse_kernel(n_team, n_rep, features_in, degree_in, blocks_in, cols_in, count_in,
-                   out1, out2, out3, features, degree, blocks, block_cols, block_count,
-                   sent, gathered, adjacency, scales, hops, in_sem,
-                   feat_send, feat_recv, scale_send, scale_recv, adj_send, adj_recv,
+                   out, features, degree, blocks, block_cols, block_count,
+                   sent, arrived, gathered, adjacency, hops, in_sem,
+                   feat_send, feat_recv, adj_send, adj_recv,
                    pass_send, pass_recv, hop_send, hop_recv, out_send, out_recv, keep_sem):
     groups = n_rep * PAIR
     chips = n_team // PAIR
@@ -29,7 +29,6 @@
     team, rep = lax.axis_index("team"), lax.axis_index("rep")
     chip, core = team // PAIR, lax.rem(team, PAIR)
     group = rep * PAIR + core
-    outs = (out1, out2, out3)
 
     loads = []
     for index, (src, dst) in enumerate(((features_in, features), (degree_in, degree),
@@ -60,7 +59,7 @@
 
     for copy in loads:
         copy.wait()
-    own_scale = lax.rsqrt(degree[...].astype(jnp.float32))
+    own_degree = degree[...].astype(jnp.float32)
 
     def as_column(row):
         on_diagonal = (lax.broadcasted_iota(jnp.int32, (rows, rows), 0)
@@ -68,11 +67,14 @@
         spread = jnp.where(on_diagonal, jnp.broadcast_to(row, (rows, rows)), 0.0)
         return jnp.sum(spread, axis=1, keepdims=True)
 
-    own_column = as_column(own_scale)
+    own_column = lax.rsqrt(as_column(own_degree))
+    degree_rows = jnp.broadcast_to(jnp.concatenate(
+        [own_degree, jnp.ones((1, group_width - rows), jnp.float32)], axis=1), (16, group_width))
+    degree_rows = degree_rows.astype(jnp.bfloat16)
     for index in range(groups):
         part = features[:, index * group_width:(index + 1) * group_width].astype(jnp.float32)
-        sent[index] = (own_column * part).astype(jnp.bfloat16)
-    scales[core, rep, 0:1, 0:rows] = own_scale
+        sent[index, 0:rows] = (own_column * part).astype(jnp.bfloat16)
+        sent[index, rows:rows + 16] = degree_rows
 
     for column in range(col_blocks):
         dense = jnp.zeros((block_size, block_size), jnp.float32)
@@ -84,10 +86,10 @@
 
     pl.semaphore_wait(barrier, groups - 1 + chips - 1)
 
-    feature_copies, scale_copies, adjacency_copies, pass_copies = [], [], [], []
+    feature_copies, adjacency_copies, pass_copies = [], [], []
     for step in range(1, groups):
         other, device = column_peer(step)
-        copy = remote(sent.at[other], gathered.at[0, rep, team],
+        copy = remote(sent.at[other], arrived.at[rep, core],
                       feat_send.at[step - 1], feat_recv.at[step - 1], device)
         copy.start()
         feature_copies.append(copy)
@@ -105,12 +107,7 @@
     copy = remote(adjacency_of(rep), adjacency_of(rep), pass_send.at[0], pass_recv.at[0], sibling)
     copy.start()
     pass_copies.append(copy)
-    for step in range(1, groups):
-        copy = remote(scales.at[core, rep], scales.at[core, rep],
-                      scale_send.at[step - 1], scale_recv.at[step - 1], column_peer(step)[1])
-        copy.start()
-        scale_copies.append(copy)
-    gathered[0, rep, team] = sent[group]
+    arrived[rep, core] = sent[group]
 
     panels = (lax.rem(core + 1, PAIR), core)
 
@@ -126,6 +123,8 @@
 
     for copy in feature_copies:
         copy.wait_recv()
+    for c in range(PAIR):
+        gathered[0, :, chip * PAIR + c] = arrived[:, c, 0:rows]
     hop_copies = [[send_hop(0, half) for half in range(PAIR)]]
 
     for step in range(1, n_rep):
@@ -135,10 +134,10 @@
                       pass_send.at[step], pass_recv.at[step], sibling)
         copy.start()
         pass_copies.append(copy)
-    for copy in scale_copies:
-        copy.wait_recv()
     scale_columns = [
-        jnp.concatenate([as_column(scales[c, r, 0:1, 0:rows]) for r in range(n_rep)], axis=0)
+        lax.rsqrt(jnp.concatenate(
+            [as_column(arrived[r, c, rows:rows + 16].astype(jnp.float32)[0:1, 0:rows])
+             for r in range(n_rep)], axis=0))
         for c in panels]
 
     near = team // team_run
@@ -187,22 +186,29 @@
                 gathered[hop + 1, :, chip * PAIR + c] = following.reshape(n_rep, rows, group_width)
                 hop_copies[hop + 1].append(send_hop(hop + 1, half))
             hops[hop, c] = current.reshape(n_rep, rows, group_width)
+            part = {HOPS - 2: (0, HOPS - 1), HOPS - 1: (HOPS - 1, 1)}.get(hop)
+            if part is None:
+                continue
+            share = pl.ds(*part)
+            which = hop - (HOPS - 2)
             for step in range(1, groups):
                 if step % PAIR == 1 - half:
                     other, device = column_peer(step)
-                    copy = remote(hops.at[hop, c, other // PAIR], outs[hop].at[:, mine],
-                                  out_send.at[hop, step - 1], out_recv.at[hop, step - 1], device)
+                    copy = remote(hops.at[share, c, other // PAIR], out.at[share, :, mine],
+                                  out_send.at[which, step - 1], out_recv.at[which, step - 1], device)
                     copy.start()
                     out_copies.append(copy)
-        kept = pltpu.make_async_copy(hops.at[hop, core, rep], outs[hop].at[:, mine], keep_sem.at[hop])
-        kept.start()
-        kept_copies.append(kept)
+            if half == PAIR - 1:
+                kept = pltpu.make_async_copy(hops.at[share, core, rep], out.at[share, :, mine],
+                                             keep_sem.at[which])
+                kept.start()
+                kept_copies.append(kept)
 
     for copy in out_copies:
         copy.wait_recv()
     for copy in kept_copies:
         copy.wait()
-    for copies in [feature_copies, scale_copies, adjacency_copies, pass_copies, out_copies]:
+    for copies in [feature_copies, adjacency_copies, pass_copies, out_copies]:
         for copy in copies:
             copy.wait_send()
     for halves in hop_copies:
@@ -211,8 +217,8 @@
                 copy.wait_send()
 
 
-def store_kernel(in1, in2, in3, out1, out2, out3, held, load_sem, store_sem):
-    refs = ((in1, out1), (in2, out2), (in3, out3))
+def store_kernel(results, out1, out2, out3, held, load_sem, store_sem):
+    refs = tuple((results.at[index], out) for index, out in enumerate((out1, out2, out3)))
     loads = [pltpu.make_async_copy(src, held.at[index], load_sem.at[index])
              for index, (src, dst) in enumerate(refs)]
     stores = [pltpu.make_async_copy(held.at[index], dst, store_sem.at[index])
@@ -238,28 +244,27 @@
     result = jax.ShapeDtypeStruct((rows, width), jnp.bfloat16)
     results = pl.pallas_call(
         functools.partial(diffuse_kernel, n_team, n_rep),
-        out_shape=(result,) * HOPS,
+        out_shape=jax.ShapeDtypeStruct((HOPS, rows, width), jnp.bfloat16),
         in_specs=[hbm] * 5,
-        out_specs=(hbm,) * HOPS,
+        out_specs=hbm,
         scratch_shapes=[
             pltpu.VMEM((rows, width), jnp.bfloat16),
             pltpu.VMEM((1, rows), jnp.int32),
             pltpu.VMEM(blocks.shape, jnp.bfloat16),
             pltpu.SMEM(block_cols.shape, jnp.int32),
             pltpu.SMEM(block_count.shape, jnp.int32),
-            pltpu.VMEM((groups, rows, group_width), jnp.bfloat16),
+            pltpu.VMEM((groups, rows + 16, group_width), jnp.bfloat16),
+            pltpu.VMEM((n_rep, PAIR, rows + 16, group_width), jnp.bfloat16),
             pltpu.VMEM((HOPS, n_rep, n_team, rows, group_width), jnp.bfloat16),
             pltpu.VMEM((n_rep, PAIR, col_blocks, panel, panel), jnp.bfloat16),
-            pltpu.VMEM((PAIR, n_rep, 8, LANES), jnp.float32),
             pltpu.VMEM((HOPS, PAIR, n_rep, rows, group_width), jnp.bfloat16),
             dma((5,)),
-            dma((groups - 1,)), dma((groups - 1,)),
             dma((groups - 1,)), dma((groups - 1,)),
             dma((n_rep - 1,)), dma((n_rep - 1,)),
             dma((n_rep,)), dma((n_rep,)),
             dma((HOPS, PAIR, chips - 1)), dma((HOPS, PAIR, chips - 1)),
-            dma((HOPS, groups - 1)), dma((HOPS, groups - 1)),
-            dma((HOPS,)),
+            dma((2, groups - 1)), dma((2, groups - 1)),
+            dma((2,)),
         ],
         compiler_params=pltpu.CompilerParams(
             collective_id=0, has_side_effects=True, vmem_limit_bytes=62 * 1024 * 1024),
@@ -267,11 +272,11 @@
     return pl.pallas_call(
         store_kernel,
         out_shape=(result,) * HOPS,
-        in_specs=[hbm] * HOPS,
+        in_specs=[hbm],
         out_specs=(hbm,) * HOPS,
         scratch_shapes=[pltpu.VMEM((HOPS, rows, width), jnp.bfloat16), dma((HOPS,)), dma((HOPS,))],
         compiler_params=pltpu.CompilerParams(vmem_limit_bytes=62 * 1024 * 1024),
-    )(*results)
+    )(results)
 
 
 def gather_and_scatter(features, degree, blocks, block_cols, block_count):
@@ -318,7 +323,7 @@
     rows, width = features.shape
     return (width % (n_rep * PAIR * LANES) == 0 and n_team == 4 * PAIR
             and n_team * rows == 2 * blocks.shape[-1]
-            and n_rep > 1 and blocks.shape[0] == 1 and rows % 16 == 0 and rows <= LANES
+            and n_rep > 1 and blocks.shape[0] == 1 and rows % 16 == 0 and rows < LANES
             and blocks.shape[-1] == n_rep * rows
             and blocks.shape[-1] % LANES == 0
             and n_rep * n_team * rows * n_rep * rows * 4 <= 4 * 1024 * 1024)

time: 35.3 us -> 35.2 us (level)
  no operation moved by 1% of the time
where the time goes in v4:
time: 35.2 us; the launch traced here: 34.9 us
  Pallas kernels  33.7 us (96%)
  between operations  1.29 us (4%)
    pallas_call x1, Pallas kernels, exchange_columns(): pl.pallas_call(functools.partial(diffuse_kernel, n_team, n_rep), out_shap...  32.1 us
    pallas_call x1, Pallas kernels, exchange_columns(): pl.pallas_call(store_kernel, out_shape=(result,) * HOPS, in_specs=[hbm],...  1.58 us

profile of v4, /device:TPU:0, one launch (start us, length us, event | category | flops | bytes accessed | tf_op | source)
XLA Modules:
  0.0 34.9 jit_solution(18310244379256312939)
XLA Ops:
  1.3 32.1 %shard_map.76.results = bf16[3,32,1024]{2,1,0:T(8,128)(2,1)} custom-call(bf16[32,1024]{1,0:T(8,128)(2,1)} %features_in.1, s32[1,32]{1,0:T(1,128)} %bitcast.1, bf16[1,1,2,128,128]{4,3,2,1,0:T(8,128)(2,1)} %blocks_in.1, s32[1,1,2]{2,1,0:T(1,128)} %cols_in.1, s32[1,1]{1,0:T(1,128)S(6)} %copy.8.count_in), custom_call_target="tpu_custom_call" | custom-call | tf_op jit(solution)/shard_map/pallas_call | solution.py:245
  33.4 1.6 %shard_map.77 = (bf16[32,1024]{1,0:T(8,128)(2,1)}, bf16[32,1024]{1,0:T(8,128)(2,1)}, bf16[32,1024]{1,0:T(8,128)(2,1)}) custom-call(bf16[3,32,1024]{2,1,0:T(8,128)(2,1)} %shard_map.76.results), custom_call_target="tpu_custom_call" | custom-call | tf_op jit(solution)/shard_map/pallas_call | solution.py:272

commit v5 on v4

--- a/solution.py
+++ b/solution.py
@@ -114,12 +114,12 @@
     def send_hop(hop, half):
         copies = []
         own = gathered.at[hop, :, chip * PAIR + panels[half]]
-        for step in (1, 3, 2):
+        for step in (3, 1, 2):
             copy = remote(own, own, hop_send.at[hop, half, step - 1],
                           hop_recv.at[hop, half, step - 1], plane_peer(step))
             copy.start()
             copies.append(copy)
-        return copies
+        return [copies[1], copies[0], copies[2]]
 
     for copy in feature_copies:
         copy.wait_recv()

time: 35.2 us -> 35.3 us (level)
  no operation moved by 1% of the time
where the time goes in v5:
time: 35.3 us; the launch traced here: 35.1 us
  Pallas kernels  33.8 us (96%)
  between operations  1.29 us (4%)
    pallas_call x1, Pallas kernels, exchange_columns(): pl.pallas_call(functools.partial(diffuse_kernel, n_team, n_rep), out_shap...  32.3 us
    pallas_call x1, Pallas kernels, exchange_columns(): pl.pallas_call(store_kernel, out_shape=(result,) * HOPS, in_specs=[hbm],...  1.58 us

profile of v5, /device:TPU:0, one launch (start us, length us, event | category | flops | bytes accessed | tf_op | source)
XLA Modules:
  0.0 35.1 jit_solution(10795256814595329405)
XLA Ops:
  1.3 32.3 %shard_map.76.results = bf16[3,32,1024]{2,1,0:T(8,128)(2,1)} custom-call(bf16[32,1024]{1,0:T(8,128)(2,1)} %features_in.1, s32[1,32]{1,0:T(1,128)} %bitcast.1, bf16[1,1,2,128,128]{4,3,2,1,0:T(8,128)(2,1)} %blocks_in.1, s32[1,1,2]{2,1,0:T(1,128)} %cols_in.1, s32[1,1]{1,0:T(1,128)S(6)} %copy.8.count_in), custom_call_target="tpu_custom_call" | custom-call | tf_op jit(solution)/shard_map/pallas_call | solution.py:245
  33.5 1.6 %shard_map.77 = (bf16[32,1024]{1,0:T(8,128)(2,1)}, bf16[32,1024]{1,0:T(8,128)(2,1)}, bf16[32,1024]{1,0:T(8,128)(2,1)}) custom-call(bf16[3,32,1024]{2,1,0:T(8,128)(2,1)} %shard_map.76.results), custom_call_target="tpu_custom_call" | custom-call | tf_op jit(solution)/shard_map/pallas_call | solution.py:272
